TPU v7x, 128 devices: a whole 4x4x4 slice. The times are simulated.
128 devices in a mesh: front: 16 (over x, z), grp: 8 (over y, core).
Axes of the slice: x: 4, y: 4, z: 4, core: 2. Of those that a mesh axis runs over, the one named last changes fastest.
Arguments:
- front_block: float32 [16, 16384, 1408], P('front', 'grp'), as said below
- child_blocks: float32 [16, 8, 4, 16, 1408], P('front', 'grp'), may hold values from -0.5 to 0.5
- child_rows: int32 [16, 8, 4, 16], P('front', 'grp'), may hold values from 0 to 2047
- child_dest: int32 [16, 8, 4, 1], P('front', 'grp'), may hold values from 0 to 15; in each aligned block of 4 rows (0 to 3, 4 to 7, ..., all dimensions but the last counted through in order) at most 2 rows name the same one
- panel_owner: int32 [16], P('front'), may hold values from 0 to 7
Outputs:
- panel_factor: float32 [16, 16384, 512], P('front', 'grp')
- schur_block: float32 [16, 16384, 896], P('front', 'grp')
Inputs may be any that keep to these rules, and one draw needn't show every extreme that they name: `child_dest`: among the 4 blocks of one device no front is named more than 2 times, and in every draw some device names some front exactly 2 times. `front_block`: for every front and row block, the first 512 rows' leading 512 x 512 block has a positive diagonal that dominates; other entries lie within -2.3 to 2.3.
All inputs are finite; a program needn't handle non-finite values.
Results may differ from a plain program's by a relative error of at most 0.0003.
Values sent between devices are 32-bit elements; how exact they have to be, the bound alone decides.
A program may use at most 128 MiB of HBM per device.

v0:
```python
import jax
import jax.numpy as jnp
from jax import lax
from jax.sharding import PartitionSpec as P

PB = 512
CAP = 2


def spread(array, axis, root):
    mine = lax.axis_index(axis) == root
    return lax.psum(jnp.where(mine, array, jnp.zeros_like(array)), axis)


def right_solve(factor, rows):
    return lax.linalg.triangular_solve(factor, rows, left_side=False, lower=True, transpose_a=True)


def pack_slots(values, slot_index, front_count):
    empty = jnp.zeros((front_count * CAP,) + values.shape[1:], values.dtype)
    filled = empty.at[slot_index].set(values)
    return filled.reshape((front_count, CAP) + values.shape[1:])


def local(front_block, child_blocks, child_rows, child_dest, panel_owner):
    local_rows = front_block[0]
    front_count = lax.axis_size("front")
    blocks = child_blocks[0, 0]
    row_lists = child_rows[0, 0]
    target_front = child_dest[0, 0, :, 0]
    block_count = target_front.shape[0]
    position = jnp.arange(block_count, dtype=jnp.int32)
    same_front = target_front[:, None] == target_front[None, :]
    earlier = position[None, :] < position[:, None]
    slot_index = target_front * CAP + jnp.sum((same_front & earlier).astype(jnp.int32), axis=1)
    send_rows = pack_slots(row_lists, slot_index, front_count)
    panel_cols = PB
    send_blocks = pack_slots(blocks, slot_index, front_count)
    got_blocks, got_rows = (
        lax.all_to_all(send_blocks, "front", split_axis=0, concat_axis=0, tiled=True),
        lax.all_to_all(send_rows, "front", split_axis=0, concat_axis=0, tiled=True),
    )
    flat_rows = got_rows.reshape(-1)
    local_rows = local_rows.at[flat_rows].add(got_blocks.reshape(-1, local_rows.shape[1]))
    win_cols = local_rows.shape[1] - panel_cols
    owner_index = panel_owner[0]
    is_owner = lax.axis_index("grp") == owner_index
    pivot_block = spread(local_rows[:panel_cols, :panel_cols], "grp", owner_index)
    symmetric = 0.5 * (pivot_block + pivot_block.T)
    pivot_factor = jnp.linalg.cholesky(symmetric)
    solved = right_solve(pivot_factor, local_rows[:, :panel_cols])
    window = spread(solved[panel_cols : panel_cols + win_cols], "grp", owner_index)
    schur_part = local_rows[:, panel_cols:] - jnp.dot(
        solved, window.T, precision=lax.Precision.HIGHEST
    )
    top_rows = jnp.where(is_owner, pivot_factor, solved[:panel_cols])
    panel_rows = jnp.concatenate([top_rows, solved[panel_cols:]], axis=0)
    return (panel_rows[None], schur_part[None])


def solution(mesh):
    placed = (
        P("front", "grp", None),
        P("front", "grp", None, None, None),
        P("front", "grp", None, None),
        P("front", "grp", None, None),
        P("front"),
    )
    return jax.shard_map(
        local,
        mesh=mesh,
        in_specs=placed,
        out_specs=(P("front", "grp", None), P("front", "grp", None)),
        check_vma=False,
    )
```

profile of v0, /device:TPU:0, one launch (start us, length us, event | category | flops | bytes accessed | tf_op | source)
XLA Modules:
  0.0 405.6 jit_solution(12922909138778709445)
XLA Ops:
  7.2 9.4 %copy.71 = f32[1,2048,1408]{2,1,0:T(8,128)} copy(f32[1,2048,1408]{2,1,0:T(8,128)} %param.5) | data formatting | bytes 23068672
  18.0 8.0 %all-to-all-start = ((s32[16,2,16]{2,1,0:T(2,128)}), s32[16,2,16]{2,1,0:T(2,128)S(1)}, u32[]{:S(2)}, u32[]{:S(2)}) async-start(s32[16,2,16]{2,1,0:T(2,128)} %bitcast.7), calls=%async_computation | async-start | bytes 32768 | tf_op jit(solution)/shard_map/all_to_all | solution.py:41
  26.0 1.8 broadcast_in_dim.26
  27.7 2.3 scatter_fusion
  30.1 3.5 all-to-all-done
  33.6 3.7 all-to-all-start.1
  38.1 38.4 %all-to-all-done.1 = f32[16,2,16,1408]{3,2,1,0:T(8,128)S(1)} async-done(((f32[16,2,16,1408]{3,2,1,0:T(8,128)}), f32[16,2,16,1408]{3,2,1,0:T(8,128)S(1)}, u32[]{:S(2)}, u32[]{:S(2)}) %all-to-all-start.1) | async-done | bytes 2883616 | tf_op jit(solution)/shard_map/all_to_all | solution.py:40
  76.6 14.0 %scatter_fusion.1 = f32[2048,1408]{1,0:T(8,128)} fusion(f32[2048,1408]{1,0:T(8,128)} %bitcast.75, s32[512]{0:T(512)S(1)} %bitcast.78, f32[512,1408]{1,0:T(8,128)S(1)} %bitcast.76), kind=kCustom, calls=%fused_computation.2 | custom fusion | flops 720896 | bytes 8652800 | tf_op jit(solution)/shard_map/scatter-add | solution.py:44
  93.6 60.5 %all-reduce.4.cloned.1.call-done = f32[512,512]{0,1:T(8,128)} async-done(((f32[512,512]{0,1:T(8,128)}), f32[512,512]{0,1:T(8,128)}) %all-reduce.4.cloned.1.call-update) | async-done | bytes 1048592 | tf_op jit(solution)/shard_map/psum | solution.py:12
  154.1 1.6 copy.34
  155.6 1.5 fusion.16
  157.7 11.7 %cholesky.103 = f32[128,128]{1,0:T(8,128)S(1)} custom-call(f32[128,128]{1,0:T(8,128)S(1)} %cholesky.263), custom_call_target="Cholesky" | custom-call | tf_op jit(solution)/shard_map/jit(cholesky)/cholesky | solution.py:50
  169.5 9.8 %custom-call.30 = f32[1,128,128]{1,2,0:T(8,128)S(1)} custom-call(f32[1,128,128]{2,1,0:T(8,128)S(1)} %get-tuple-element.43), custom_call_target="InvertDiagBlocksLowerTriangular" | custom-call | tf_op jit(solution)/shard_map/jit(cholesky)/cholesky | solution.py:50
  179.9 11.7 %cholesky.215 = f32[128,128]{1,0:T(8,128)S(1)} custom-call(f32[128,128]{1,0:T(8,128)S(1)} %cholesky.267), custom_call_target="Cholesky" | custom-call | tf_op jit(solution)/shard_map/jit(cholesky)/cholesky | solution.py:50
  192.2 10.2 %custom-call.31 = f32[1,128,128]{1,2,0:T(8,128)S(1)} custom-call(f32[1,128,128]{2,1,0:T(8,128)S(1)} %get-tuple-element.41), custom_call_target="InvertDiagBlocksLowerTriangular" | custom-call | tf_op jit(solution)/shard_map/jit(cholesky)/cholesky | solution.py:50
  203.3 11.7 %cholesky.236 = f32[128,128]{1,0:T(8,128)S(1)} custom-call(f32[128,128]{1,0:T(8,128)S(1)} %cholesky.272), custom_call_target="Cholesky" | custom-call | tf_op jit(solution)/shard_map/jit(cholesky)/cholesky | solution.py:50
  215.2 9.8 %custom-call.32 = f32[1,128,128]{1,2,0:T(8,128)S(1)} custom-call(f32[1,128,128]{2,1,0:T(8,128)S(1)} %get-tuple-element.39), custom_call_target="InvertDiagBlocksLowerTriangular" | custom-call | tf_op jit(solution)/shard_map/jit(cholesky)/cholesky | solution.py:50
  225.8 11.9 %cholesky.253 = f32[128,128]{1,0:T(8,128)S(1)} custom-call(f32[128,128]{1,0:T(8,128)S(1)} %convolution_subtract_fusion.4), custom_call_target="Cholesky" | custom-call | tf_op jit(solution)/shard_map/jit(cholesky)/cholesky | solution.py:50
  242.7 10.8 %while.1 = (s32[]{:T(128)}, f32[512,512]{0,1:T(8,128)S(1)}, s32[4,2]{0,1:T(2,128)S(1)}, f32[4,128,128]{2,1,0:T(8,128)}, s32[]{:T(128)}) while((s32[]{:T(128)}, f32[512,512]{0,1:T(8,128)S(1)}, s32[4,2]{0,1:T(2,128)S(1)}, f32[4,128,128]{2,1,0:T(8,128)}, s32[]{:T(128)}) %tuple.33), condition=%wide.while_cond, body=%wide.while_body.sunk | while | flops 2 | bytes 393829 | solution.py:16
  246.0 1.3 dynamic-slice.7
  248.7 1.3 dynamic-slice.7
  253.4 40.2 %custom-call.33 = f32[4,128,128]{1,2,0:T(8,128)S(1)} custom-call(f32[4,128,128]{2,1,0:T(8,128)} %get-tuple-element.9), custom_call_target="InvertDiagBlocksLowerTriangular" | custom-call | tf_op jit(solution)/shard_map/triangular_solve | solution.py:16
  293.6 2.3 fusion.13
  295.9 3.0 convolution_subtract_fusion.1
  300.1 4.8 %convolution_subtract_fusion = f32[2048,128]{1,0:T(8,128)S(1)} fusion(f32[2048,128]{0,1:T(8,128)S(1)} %fusion.28, f32[2048,128]{0,1:T(8,128)S(1)} %fusion.13, f32[2048,1408]{1,0:T(8,128)} %scatter_fusion.1, f32[512,512]{0,1:T(8,128)S(1)} %get-tuple-element.98), kind=kOutput, calls=%fused_computation.16 | convolution fusion | flops 806092800 | bytes 4325376 | tf_op jit(solution)/shard_map/triangular_solve | solution.py:16
  306.0 7.0 %fusion.7 = f32[2048,128]{1,0:T(8,128)S(1)} fusion(f32[2048,128]{0,1:T(8,128)S(1)} %fusion.27, f32[2048,128]{0,1:T(8,128)S(1)} %fusion.28, f32[2048,128]{0,1:T(8,128)S(1)} %fusion.13, f32[2048,1408]{1,0:T(8,128)} %scatter_fusion.1, f32[512,512]{0,1:T(8,128)} %copy-done.6), kind=kOutput, calls=%fused_computation.15 | convolution fusion | flops 1209794560 | bytes 5439488 | tf_op jit(solution)/shard_map/triangular_solve | solution.py:16
  315.1 1.4 maximum_select_fusion
  316.6 1.7 pad_maximum_fusion
  320.1 2.4 maximum_bitcast_fusion
  322.4 5.4 %copy.44 = f32[1,2048,512]{2,1,0:T(8,128)} copy(f32[1,2048,512]{1,2,0:T(8,128)} %maximum_bitcast_fusion) | data formatting | bytes 8388608
  327.8 53.1 %all-reduce.6.cloned.1.call-done = f32[896,512]{0,1:T(8,128)} async-done(((f32[896,512]{0,1:T(8,128)}), f32[896,512]{0,1:T(8,128)}) %all-reduce.6.cloned.1.call-update) | async-done | bytes 1835024 | tf_op jit(solution)/shard_map/psum | solution.py:12
  380.9 17.7 %fusion = f32[1,2048,896]{2,1,0:T(8,128)} fusion(f32[2048,1408]{1,0:T(8,128)} %scatter_fusion.1, f32[896,512]{0,1:T(8,128)} %all-reduce.6.cloned.1.call-done, f32[2048,128]{0,1:T(8,128)} %copy-done.2, f32[2048,128]{0,1:T(8,128)S(1)} %fusion.27, f32[2048,128]{0,1:T(8,128)S(1)} %fusion.28, f32[2048,128]{0,1:T(8,128)S(1)} %fusion.13), kind=kOutput, calls=%fused_computation.6 | convolution fusion | flops 11279269888 | bytes 20709376 | tf_op jit(solution)/shard_map/dot_general | solution.py:53
  (85 shorter events, 24.5 us)
Async XLA Ops:
  7.2 9.7 %copy-start = (s32[1,1,4,16]{3,2,1,0:T(4,128)S(1)}, s32[1,1,4,16]{3,2,1,0:T(4,128)}, u32[]{:S(2)}) copy-start(s32[1,1,4,16]{3,2,1,0:T(4,128)} %param.7) | copy-start | bytes 772
  7.2 20.6 %copy-start.7 = (f32[1,1,4,16,1408]{4,3,2,1,0:T(8,128)S(1)}, f32[1,1,4,16,1408]{4,3,2,1,0:T(8,128)}, u32[]{:S(2)}) copy-start(f32[1,1,4,16,1408]{4,3,2,1,0:T(8,128)} %param.6) | copy-start | bytes 1081348
  7.2 9.4 %copy-start.8 = (s32[1,1,4,1]{2,3,1,0:T(1,128)S(1)}, s32[1,1,4,1]{2,3,1,0:T(1,128)}, u32[]{:S(2)}) copy-start(s32[1,1,4,1]{2,3,1,0:T(1,128)} %param.8) | copy-start | bytes 52
  18.0 15.6 %all-to-all-start = ((s32[16,2,16]{2,1,0:T(2,128)}), s32[16,2,16]{2,1,0:T(2,128)S(1)}, u32[]{:S(2)}, u32[]{:S(2)}) async-start(s32[16,2,16]{2,1,0:T(2,128)} %bitcast.7), calls=%async_computation | async-start | bytes 32768 | tf_op jit(solution)/shard_map/all_to_all | solution.py:41
  33.6 43.0 %all-to-all-start.1 = ((f32[16,2,16,1408]{3,2,1,0:T(8,128)}), f32[16,2,16,1408]{3,2,1,0:T(8,128)S(1)}, u32[]{:S(2)}, u32[]{:S(2)}) async-start(f32[16,2,16,1408]{3,2,1,0:T(8,128)} %bitcast.10), calls=%async_computation.1 | async-start | bytes 5767168 | tf_op jit(solution)/shard_map/all_to_all | solution.py:40
  37.3 116.8 %all-reduce.4.cloned.1.call-start = ((), (), s32[]{:S(2)}) async-start(), calls=%async_computation.2 | async-start | bytes 2097152 | tf_op jit(solution)/shard_map/psum | solution.py:12
  93.3 287.6 %all-reduce.6.cloned.1.call-start = ((), (), s32[]{:S(2)}) async-start(), calls=%async_computation.3 | async-start | bytes 3670016 | tf_op jit(solution)/shard_map/psum | solution.py:12
  239.2 14.3 %copy-start.4 = (f32[512,512]{0,1:T(8,128)}, f32[512,512]{0,1:T(8,128)S(1)}, u32[]{:S(2)}) copy-start(f32[512,512]{0,1:T(8,128)S(1)} %constant_dynamic-update-slice_fusion.1) | copy-start | bytes 3145732
  253.4 46.6 %copy-start.6 = (f32[512,512]{0,1:T(8,128)}, f32[512,512]{0,1:T(8,128)S(1)}, u32[]{:S(2)}) copy-start(f32[512,512]{0,1:T(8,128)S(1)} %get-tuple-element.98) | copy-start | bytes 3145732
  314.1 1.0 copy-start.2
  318.3 1.2 copy-start.3
  318.3 1.5 copy-start.5
  380.9 17.7 %copy-start.1 = (s32[1,1,4,16]{3,2,1,0:T(4,128)S(1)}, s32[1,1,4,16]{3,2,1,0:T(4,128)}, u32[]{:S(2)}) copy-start(s32[1,1,4,16]{3,2,1,0:T(4,128)} %param.7) | copy-start | bytes 772
Sparse Core Ops, SparseCore 0:
  93.4 60.5 all-reduce.3
  316.7 64.1 all-reduce.5
where the time goes:
time: 412 us; the launch traced here: 406 us
  waiting for transfers between devices  156 us (38%)
  other arithmetic  142 us (34%)
  matrix products  40.4 us (10%)
  local copies, waits for them, and re-layouts  37.6 us (9%)
  between operations  17.9 us (4%)
  starting transfers between devices  12 us (3%)
    psum x2, waiting for transfers between devices, spread(): return lax.psum(jnp.where(mine, array, jnp.zeros_like(array)), axis)  114 us
    another operation x14, other arithmetic, local(): pivot_factor = jnp.linalg.cholesky(symmetric)  79.1 us
    another operation x4, other arithmetic, right_solve(): lax.linalg.triangular_solve(factor, rows, left_side=False, lower=True, tr...  42 us
    all_to_all x1, waiting for transfers between devices, local(): lax.all_to_all(send_blocks, 'front', split_axis=0, concat_axis=0, tiled=T...  38.4 us
    another operation x7, matrix products, right_solve(): lax.linalg.triangular_solve(factor, rows, left_side=False, lower=True, tr...  20.5 us
    dot_general x1, matrix products, local(): jnp.dot(solved, window.T, precision=lax.Precision.HIGHEST)  17.7 us
    unnamed x21, local copies, waits for them, and re-layouts  17.4 us
    scatter-add x1, other arithmetic, local(): local_rows.at[flat_rows].add(got_blocks.reshape(-1, local_rows.shape[1]))  14 us
  transfers between devices with their start and end apart: 4, of which 4 were waited for; matrix products, arithmetic and copies ran while one was open for 3% of the time, Pallas kernels for 0%

commit v1 on v0

--- a/solution.py
+++ b/solution.py
@@ -9,7 +9,7 @@
 
 def spread(array, axis, root):
     mine = lax.axis_index(axis) == root
-    return lax.psum(jnp.where(mine, array, jnp.zeros_like(array)), axis)
+    return jnp.sum(lax.all_gather(jnp.where(mine, array, jnp.zeros_like(array)), axis), axis=0)
 
 
 def right_solve(factor, rows):

time: 412 us -> 427 us (1.036)
  other arithmetic: 142 us -> 155 us
  local copies, waits for them, and re-layouts: 37.6 us -> 32.5 us
    all_gather x0 -> x2, waiting for transfers between devices: none -> 118 us  [spread(): lax.all_gather(jnp.where(mine, array, jnp.zeros_like(array)), axis)]
    psum x2 -> x0, waiting for transfers between devices: 114 us -> none  [spread(): return lax.psum(jnp.where(mine, array, jnp.zeros_like(array)), axis)]
    reduce_sum x0 -> x2, other arithmetic: none -> 13 us  [spread(): jnp.sum(lax.all_gather(jnp.where(mine, array, jnp.zeros_like(array)), axi...]
    unnamed x21 -> x23, local copies, waits for them, and re-layouts: 17.4 us -> 12.5 us
    another operation x20 -> x12, local copies, waits for them, and re-layouts: 10.7 us -> 10.4 us
  transfers between devices with their start and end apart: 4 -> 4, of which waited for: 4 -> 4; matrix products, arithmetic and copies ran while one was open for 3% -> 2% of each run, Pallas kernels for 0% -> 0%
where the time goes in v1:
time: 427 us; the launch traced here: 420 us
  waiting for transfers between devices  160 us (37%)
  other arithmetic  155 us (36%)
  matrix products  42.9 us (10%)
  local copies, waits for them, and re-layouts  32.5 us (8%)
  between operations  17.7 us (4%)
  starting transfers between devices  12 us (3%)
    all_gather x2, waiting for transfers between devices, spread(): lax.all_gather(jnp.where(mine, array, jnp.zeros_like(array)), axis)  118 us
    another operation x14, other arithmetic, local(): pivot_factor = jnp.linalg.cholesky(symmetric)  79 us
    another operation x4, other arithmetic, right_solve(): lax.linalg.triangular_solve(factor, rows, left_side=False, lower=True, tr...  41.9 us
    all_to_all x1, waiting for transfers between devices, local(): lax.all_to_all(send_blocks, 'front', split_axis=0, concat_axis=0, tiled=T...  38.4 us
    another operation x7, matrix products, right_solve(): lax.linalg.triangular_solve(factor, rows, left_side=False, lower=True, tr...  23.9 us
    dot_general x1, matrix products, local(): jnp.dot(solved, window.T, precision=lax.Precision.HIGHEST)  17.2 us
    scatter-add x1, other arithmetic, local(): local_rows.at[flat_rows].add(got_blocks.reshape(-1, local_rows.shape[1]))  13.9 us
    reduce_sum x2, other arithmetic, spread(): jnp.sum(lax.all_gather(jnp.where(mine, array, jnp.zeros_like(array)), axi...  13 us
  transfers between devices with their start and end apart: 4, of which 4 were waited for; matrix products, arithmetic and copies ran while one was open for 2% of the time, Pallas kernels for 0%

profile of v1, /device:TPU:0, one launch (start us, length us, event | category | flops | bytes accessed | tf_op | source)
XLA Modules:
  0.0 420.1 jit_solution(14278534969747527827)
XLA Ops:
  7.2 9.3 %copy.41 = f32[1,2048,1408]{2,1,0:T(8,128)} copy(f32[1,2048,1408]{2,1,0:T(8,128)} %param.5) | data formatting | bytes 23068672
  17.9 8.0 %all-to-all-start = ((s32[16,2,16]{2,1,0:T(2,128)}), s32[16,2,16]{2,1,0:T(2,128)S(1)}, u32[]{:S(2)}, u32[]{:S(2)}) async-start(s32[16,2,16]{2,1,0:T(2,128)} %bitcast.7), calls=%async_computation | async-start | bytes 32768 | tf_op jit(solution)/shard_map/all_to_all | solution.py:41
  27.6 2.3 scatter_fusion
  30.0 3.5 all-to-all-done
  33.5 3.7 all-to-all-start.1
  38.0 38.4 %all-to-all-done.1 = f32[16,2,16,1408]{3,2,1,0:T(8,128)S(1)} async-done(((f32[16,2,16,1408]{3,2,1,0:T(8,128)}), f32[16,2,16,1408]{3,2,1,0:T(8,128)S(1)}, u32[]{:S(2)}, u32[]{:S(2)}) %all-to-all-start.1) | async-done | bytes 2883616 | tf_op jit(solution)/shard_map/all_to_all | solution.py:40
  76.5 13.9 %scatter_fusion.1 = f32[2048,1408]{1,0:T(8,128)} fusion(f32[2048,1408]{1,0:T(8,128)} %bitcast.79, s32[512]{0:T(512)S(1)} %bitcast.84, f32[512,1408]{1,0:T(8,128)S(1)} %bitcast.81), kind=kCustom, calls=%fused_computation.2 | custom fusion | flops 720896 | bytes 8652800 | tf_op jit(solution)/shard_map/scatter-add | solution.py:44
  90.4 2.3 slice_select_fusion
  92.9 47.8 %all-gather.5.cloned.1.call-done = f32[4096,512]{1,0:T(8,128)} async-done(((f32[512,512]{1,0:T(8,128)}), f32[4096,512]{1,0:T(8,128)}) %all-gather.5.cloned.1.call-update) | async-done | bytes 8388624 | tf_op jit(solution)/shard_map/all_gather | solution.py:12
  140.7 4.5 %reduce_sum.31 = f32[512,512]{1,0:T(8,128)S(1)} reduce(f32[8,512,512]{2,1,0:T(8,128)} %bitcast.82, f32[]{:T(128)} %constant.156.clone.1), dimensions={0}, to_apply=%region_4.5 | reduce | flops 1835008 | bytes 9437188 | tf_op jit(solution)/shard_map/reduce_sum | solution.py:12
  145.9 11.7 %cholesky.103 = f32[128,128]{1,0:T(8,128)S(1)} custom-call(f32[128,128]{1,0:T(8,128)S(1)} %cholesky.263), custom_call_target="Cholesky" | custom-call | tf_op jit(solution)/shard_map/jit(cholesky)/cholesky | solution.py:50
  157.8 9.8 %custom-call.30 = f32[1,128,128]{1,2,0:T(8,128)S(1)} custom-call(f32[1,128,128]{2,1,0:T(8,128)S(1)} %get-tuple-element.29), custom_call_target="InvertDiagBlocksLowerTriangular" | custom-call | tf_op jit(solution)/shard_map/jit(cholesky)/cholesky | solution.py:50
  168.2 12.1 %cholesky.215 = f32[128,128]{1,0:T(8,128)S(1)} custom-call(f32[128,128]{1,0:T(8,128)S(1)} %cholesky.267), custom_call_target="Cholesky" | custom-call | tf_op jit(solution)/shard_map/jit(cholesky)/cholesky | solution.py:50
  180.4 9.8 %custom-call.31 = f32[1,128,128]{1,2,0:T(8,128)S(1)} custom-call(f32[1,128,128]{2,1,0:T(8,128)S(1)} %get-tuple-element.26), custom_call_target="InvertDiagBlocksLowerTriangular" | custom-call | tf_op jit(solution)/shard_map/jit(cholesky)/cholesky | solution.py:50
  190.9 11.7 %cholesky.236 = f32[128,128]{1,0:T(8,128)S(1)} custom-call(f32[128,128]{1,0:T(8,128)S(1)} %cholesky.272), custom_call_target="Cholesky" | custom-call | tf_op jit(solution)/shard_map/jit(cholesky)/cholesky | solution.py:50
  203.3 9.8 %custom-call.32 = f32[1,128,128]{1,2,0:T(8,128)S(1)} custom-call(f32[1,128,128]{2,1,0:T(8,128)S(1)} %get-tuple-element.23), custom_call_target="InvertDiagBlocksLowerTriangular" | custom-call | tf_op jit(solution)/shard_map/jit(cholesky)/cholesky | solution.py:50
  213.7 11.9 %cholesky.253 = f32[128,128]{1,0:T(8,128)S(1)} custom-call(f32[128,128]{1,0:T(8,128)S(1)} %convolution_subtract_fusion.4), custom_call_target="Cholesky" | custom-call | tf_op jit(solution)/shard_map/jit(cholesky)/cholesky | solution.py:50
  229.6 10.4 %while.1 = (s32[]{:T(128)}, f32[512,512]{1,0:T(8,128)S(1)}, s32[4,2]{0,1:T(2,128)S(1)}, f32[4,128,128]{2,1,0:T(8,128)}, s32[]{:T(128)}) while((s32[]{:T(128)}, f32[512,512]{1,0:T(8,128)S(1)}, s32[4,2]{0,1:T(2,128)S(1)}, f32[4,128,128]{2,1,0:T(8,128)}, s32[]{:T(128)}) %tuple.31), condition=%wide.while_cond, body=%wide.while_body.sunk | while | flops 2 | bytes 132205 | solution.py:16
  230.2 2.0 bitcast_dynamic-update-slice_fusion.2
  232.8 2.0 bitcast_dynamic-update-slice_fusion.2
  235.4 2.0 bitcast_dynamic-update-slice_fusion.2
  240.0 40.2 %custom-call.33 = f32[4,128,128]{1,2,0:T(8,128)S(1)} custom-call(f32[4,128,128]{2,1,0:T(8,128)} %get-tuple-element.9), custom_call_target="InvertDiagBlocksLowerTriangular" | custom-call | tf_op jit(solution)/shard_map/triangular_solve | solution.py:16
  280.2 2.3 fusion.13
  282.9 3.1 convolution_subtract_fusion.1
  286.0 2.1 fusion.28
  289.6 5.2 %convolution_subtract_fusion = f32[2048,128]{1,0:T(8,128)S(1)} fusion(f32[2048,128]{0,1:T(8,128)} %fusion.28, f32[2048,128]{0,1:T(8,128)S(1)} %fusion.13, f32[2048,1408]{1,0:T(8,128)} %scatter_fusion.1, f32[512,512]{1,0:T(8,128)} %copy-done.8), kind=kOutput, calls=%fused_computation.16 | convolution fusion | flops 806092800 | bytes 4325376 | tf_op jit(solution)/shard_map/triangular_solve | solution.py:16
  296.9 7.9 %fusion.7 = f32[2048,128]{1,0:T(8,128)} fusion(f32[2048,128]{0,1:T(8,128)S(1)} %fusion.27, f32[2048,128]{0,1:T(8,128)S(1)} %copy-done.4, f32[2048,128]{0,1:T(8,128)S(1)} %fusion.13, f32[2048,1408]{1,0:T(8,128)} %scatter_fusion.1, f32[512,512]{1,0:T(8,128)} %copy-done.8), kind=kOutput, calls=%fused_computation.15 | convolution fusion | flops 1209794560 | bytes 5439488 | tf_op jit(solution)/shard_map/triangular_solve | solution.py:16
  306.4 2.2 fusion.26
  314.3 2.5 maximum_bitcast_fusion
  316.8 70.7 %all-gather.7.cloned.1.call-done = f32[7168,512]{1,0:T(8,128)} async-done(((f32[896,512]{1,0:T(8,128)}), f32[7168,512]{1,0:T(8,128)}) %all-gather.7.cloned.1.call-update) | async-done | bytes 14680080 | tf_op jit(solution)/shard_map/all_gather | solution.py:12
  387.5 8.4 %reduce_sum.32 = f32[896,512]{1,0:T(8,128)} reduce(f32[8,896,512]{2,1,0:T(8,128)} %bitcast.80, f32[]{:T(128)} %constant.156.clone.1), dimensions={0}, to_apply=%region_13.14 | reduce | flops 3211264 | bytes 16515076 | tf_op jit(solution)/shard_map/reduce_sum | solution.py:12
  395.9 17.2 %fusion = f32[1,2048,896]{2,1,0:T(8,128)} fusion(f32[2048,1408]{1,0:T(8,128)} %scatter_fusion.1, f32[896,512]{1,0:T(8,128)} %reduce_sum.32, f32[2048,128]{1,0:T(8,128)} %copy-done.2, f32[2048,128]{1,0:T(8,128)S(1)} %copy.20, f32[2048,128]{1,0:T(8,128)S(1)} %copy.19, f32[2048,128]{1,0:T(8,128)S(1)} %copy.18), kind=kOutput, calls=%fused_computation.6 | convolution fusion | flops 11279269888 | bytes 20709376 | tf_op jit(solution)/shard_map/dot_general | solution.py:53
  (72 shorter events, 24.1 us)
Async XLA Ops:
  7.2 9.6 %copy-start = (s32[1,1,4,16]{3,2,1,0:T(4,128)S(1)}, s32[1,1,4,16]{3,2,1,0:T(4,128)}, u32[]{:S(2)}) copy-start(s32[1,1,4,16]{3,2,1,0:T(4,128)} %param.7) | copy-start | bytes 772
  7.2 9.3 %copy-start.10 = (s32[1,1,4,1]{2,3,1,0:T(1,128)S(1)}, s32[1,1,4,1]{2,3,1,0:T(1,128)}, u32[]{:S(2)}) copy-start(s32[1,1,4,1]{2,3,1,0:T(1,128)} %param.8) | copy-start | bytes 52
  7.2 20.4 %copy-start.9 = (f32[1,1,4,16,1408]{4,3,2,1,0:T(8,128)S(1)}, f32[1,1,4,16,1408]{4,3,2,1,0:T(8,128)}, u32[]{:S(2)}) copy-start(f32[1,1,4,16,1408]{4,3,2,1,0:T(8,128)} %param.6) | copy-start | bytes 1081348
  17.9 15.6 %all-to-all-start = ((s32[16,2,16]{2,1,0:T(2,128)}), s32[16,2,16]{2,1,0:T(2,128)S(1)}, u32[]{:S(2)}, u32[]{:S(2)}) async-start(s32[16,2,16]{2,1,0:T(2,128)} %bitcast.7), calls=%async_computation | async-start | bytes 32768 | tf_op jit(solution)/shard_map/all_to_all | solution.py:41
  33.5 43.0 %all-to-all-start.1 = ((f32[16,2,16,1408]{3,2,1,0:T(8,128)}), f32[16,2,16,1408]{3,2,1,0:T(8,128)S(1)}, u32[]{:S(2)}, u32[]{:S(2)}) async-start(f32[16,2,16,1408]{3,2,1,0:T(8,128)} %bitcast.10), calls=%async_computation.1 | async-start | bytes 5767168 | tf_op jit(solution)/shard_map/all_to_all | solution.py:40
  37.2 103.5 %all-gather.5.cloned.1.call-start = ((), (), s32[]{:S(2)}) async-start(), calls=%async_computation.2 | async-start | bytes 9437184 | tf_op jit(solution)/shard_map/all_gather | solution.py:12
  92.7 294.8 %all-gather.7.cloned.1.call-start = ((), (), s32[]{:S(2)}) async-start(), calls=%async_computation.3 | async-start | bytes 16515072 | tf_op jit(solution)/shard_map/all_gather | solution.py:12
  225.6 54.6 %copy-start.5 = (f32[512,512]{1,0:T(8,128)}, f32[512,512]{1,0:T(8,128)S(1)}, u32[]{:S(2)}) copy-start(f32[512,512]{1,0:T(8,128)S(1)} %get-tuple-element.21) | copy-start | bytes 3145732
  240.0 42.5 %copy-start.8 = (f32[512,512]{1,0:T(8,128)}, f32[512,512]{1,0:T(8,128)S(1)}, u32[]{:S(2)}) copy-start(f32[512,512]{1,0:T(8,128)S(1)} %get-tuple-element.87) | copy-start | bytes 3145732
  289.6 7.3 %copy-start.4 = (f32[2048,128]{0,1:T(8,128)S(1)}, f32[2048,128]{0,1:T(8,128)}, u32[]{:S(2)}) copy-start(f32[2048,128]{0,1:T(8,128)} %fusion.28) | copy-start | bytes 3145732
  295.9 1.0 copy-start.7
  308.6 1.0 copy-start.2
  312.6 1.2 copy-start.3
  312.6 1.5 copy-start.6
  395.9 17.2 %copy-start.1 = (s32[1,1,4,16]{3,2,1,0:T(4,128)S(1)}, s32[1,1,4,16]{3,2,1,0:T(4,128)}, u32[]{:S(2)}) copy-start(s32[1,1,4,16]{3,2,1,0:T(4,128)} %param.7) | copy-start | bytes 772
Sparse Core Ops, SparseCore 0:
  92.8 47.8 all-gather.4
  311.1 76.3 all-gather.6
